TPU v7x, 128 devices: a whole 4x4x4 slice. The times are simulated.
128 devices in a mesh: pool: 8 (over z, y_hi), seq: 16 (over x, y_lo, core).
Axes of the slice: x: 4, y: 4 (y_hi: 2, y_lo: 2; y = y_hi * 2 + y_lo), z: 4, core: 2. Of those that a mesh axis runs over, the one named last changes fastest.
Arguments:
- patches: bfloat16 [8192, 1280], P(('pool', 'seq')), may hold values from -6 to 6
- merge_up: bfloat16 [5120, 5120], P(None, 'seq'), may hold values from -0.078125 to 0.078125
- merge_down: bfloat16 [5120, 8192], P('seq'), may hold values from -0.078125 to 0.078125
- image_pos: int32 [2048], P(('pool', 'seq')), may hold values from 0 to 6143, as said below
- text_rows: bfloat16 [6144, 8192], P('seq'), may hold values from -6 to 6
- segment: int32 [6144], P('seq'), may hold values from 0 to 3, never falling along the last dimension, each value on 1 to 4608 neighbouring positions
- query_weight: bfloat16 [8192, 8192], P('seq', 'pool')
- key_weight: bfloat16 [8192, 1024], P('seq', 'pool')
- value_weight: bfloat16 [8192, 1024], P('seq', 'pool'), may hold values from -0.0625 to 0.0625
Outputs:
- attended: bfloat16 [6144, 8192], P('seq', 'pool')
Inputs may be any that keep to these rules, and one draw needn't show every extreme that they name: `image_pos`: positions are all distinct. Of the 16 image tokens of one device, at most 2 lie in one block of 384 positions, and in every device's tokens some block holds exactly 2. `segment`: request numbers never fall along the sequence.
All inputs are finite; a program needn't handle non-finite values.
Results may differ from a plain program's by a relative error of at most 0.02.
The roundings to bfloat16 on the way count: a program that leaves them out, or rounds other values in their place, can miss the bound.
Values may be sent and summed in bfloat16 or wider, within the bound.
No kernel may reach another device: no remote copies, remote signals or barrier semaphores. Data moves between devices by JAX's collectives and lax.ppermute only.
A program may use at most 128 MiB of HBM per device.

v0:
```python
import jax
import jax.numpy as jnp
from jax import lax
from jax.sharding import PartitionSpec as P

HD = 128
CAP = 2


NORM_EPS = 1e-06
ROPE_BASE = 1000000.0


def rms_rows(matrix):
    return matrix * lax.rsqrt(jnp.mean(matrix * matrix, axis=-1, keepdims=True) + NORM_EPS)


def rotate(tensor, positions):
    half_width = tensor.shape[-1] // 2
    frequency = ROPE_BASE ** (-(jnp.arange(half_width, dtype=jnp.float32) * 2.0 / tensor.shape[-1]))
    angles = positions.astype(jnp.float32)[:, None] * frequency[None, :]
    cosine = jnp.cos(angles)[:, None, :]
    sine_part = jnp.sin(angles)[:, None, :]
    first = tensor[..., :half_width]
    second = tensor[..., half_width:]
    return jnp.concatenate(
        [first * cosine - second * sine_part, second * cosine + first * sine_part], axis=-1
    )


def per_device(
    patches,
    merge_up,
    merge_down,
    image_pos,
    text_rows,
    segment,
    query_weight,
    key_weight,
    value_weight,
):
    seq_count = lax.axis_size("seq")
    seq_index = lax.axis_index("seq")
    tok_rows = text_rows.shape[0]
    model_width = text_rows.shape[1]
    normed = rms_rows(patches.astype(jnp.float32)).astype(jnp.bfloat16)
    merged = normed.reshape(-1, 4 * patches.shape[1])
    hidden = jax.nn.gelu(
        jnp.dot(
            lax.all_gather(merged, "seq", axis=0, tiled=True),
            merge_up,
            preferred_element_type=jnp.float32,
        ),
        approximate=False,
    ).astype(jnp.bfloat16)
    image_rows = lax.psum_scatter(
        jnp.dot(hidden, merge_down, preferred_element_type=jnp.float32),
        "seq",
        scatter_dimension=0,
        tiled=True,
    ).astype(jnp.bfloat16)
    target = image_pos // tok_rows
    offset = image_pos % tok_rows
    matches = (target[:, None] == jnp.arange(seq_count, dtype=jnp.int32)[None, :]).astype(jnp.int32)
    slot_rank = jnp.sum((jnp.cumsum(matches, axis=0) - matches) * matches, axis=1)
    slot_index = target * CAP + slot_rank
    select = slot_index[None, :] == jnp.arange(seq_count * CAP, dtype=jnp.int32)[:, None]
    send_rows = jnp.dot(
        select.astype(jnp.bfloat16), image_rows, preferred_element_type=jnp.float32
    ).astype(jnp.bfloat16)
    send_rows = send_rows.reshape(seq_count, CAP, model_width)
    send_offsets = (jnp.sum(jnp.where(select, offset[None, :] + 1, 0), axis=1) - 1).reshape(
        seq_count, CAP
    )
    got_rows, got_offsets = (
        lax.all_to_all(send_rows, "seq", split_axis=0, concat_axis=0, tiled=True),
        lax.all_to_all(send_offsets, "seq", split_axis=0, concat_axis=0, tiled=True),
    )
    all_rows, all_offsets = (
        lax.all_gather(got_rows, "pool", axis=0, tiled=True),
        lax.all_gather(got_offsets, "pool", axis=0, tiled=True),
    )
    flat_rows = all_rows.reshape(-1, model_width)
    flat_offsets = all_offsets.reshape(-1)
    placed_at = jnp.where(flat_offsets >= 0, flat_offsets, tok_rows)
    seq_rows = text_rows.at[placed_at].set(flat_rows, mode="drop")
    xnorm = rms_rows(seq_rows.astype(jnp.float32)).astype(jnp.bfloat16)
    pieces = (
        lax.all_gather(query_weight, "seq", axis=0, tiled=True),
        lax.all_gather(key_weight, "seq", axis=0, tiled=True),
        lax.all_gather(value_weight, "seq", axis=0, tiled=True),
    )
    query_sum, key_sum, value_sum = tuple(
        (
            jnp.dot(xnorm, weight_piece, preferred_element_type=jnp.float32)
            for weight_piece in pieces
        )
    )
    heads_local = query_weight.shape[1] // HD
    kv_local = key_weight.shape[1] // HD
    group_size = heads_local // kv_local
    positions = seq_index * tok_rows + jnp.arange(tok_rows, dtype=jnp.int32)
    queries = rotate(query_sum.reshape(tok_rows, heads_local, HD), positions).astype(jnp.bfloat16)
    queries = queries.reshape(tok_rows, kv_local, group_size, HD)
    key_rows = (
        rotate(key_sum.reshape(tok_rows, kv_local, HD), positions)
        .astype(jnp.bfloat16)
        .reshape(tok_rows, kv_local * HD)
    )
    values = value_sum.astype(jnp.bfloat16)
    score_scale = HD ** (-0.5)

    def block_update(carried, key_block, value_block, segment_block, key_start):
        running_max, denominator, weighted = carried
        row_count = key_block.shape[0]
        key_positions = key_start + jnp.arange(row_count, dtype=jnp.int32)
        allowed = (key_positions[None, :] <= positions[:, None]) & (
            segment_block[None, :] == segment[:, None]
        )
        scores = (
            jnp.einsum(
                "tkgd,skd->kgts",
                queries,
                key_block.reshape(row_count, kv_local, HD),
                preferred_element_type=jnp.float32,
            )
            * score_scale
        )
        scores = jnp.where(allowed[None, None], scores, -1e30)
        new_max = jnp.maximum(running_max, jnp.max(scores, axis=-1))
        weights = jnp.where(allowed[None, None], jnp.exp(scores - new_max[..., None]), 0.0)
        factor = jnp.exp(running_max - new_max)
        denominator = denominator * factor + jnp.sum(weights, axis=-1)
        weighted = weighted * factor[..., None] + jnp.einsum(
            "kgts,skd->kgtd",
            weights.astype(jnp.bfloat16),
            value_block.reshape(row_count, kv_local, HD),
            preferred_element_type=jnp.float32,
        )
        return (new_max, denominator, weighted)

    def key_step(carried, key_block, value_block, segment_block, key_start):
        return block_update(carried, key_block, value_block, segment_block, key_start)

    start_state = (
        jnp.full((kv_local, group_size, tok_rows), -1e30, jnp.float32),
        jnp.zeros((kv_local, group_size, tok_rows), jnp.float32),
        jnp.zeros((kv_local, group_size, tok_rows, HD), jnp.float32),
    )
    key_piece = lax.all_gather(key_rows, "seq", axis=0, tiled=True)
    value_piece = lax.all_gather(values, "seq", axis=0, tiled=True)
    segment_piece = lax.all_gather(segment, "seq", axis=0, tiled=True)
    row_count = key_piece.shape[0]
    block_rows = 512
    block_count = row_count // block_rows

    def inner_step(kept, block_items):
        key_block, value_block, segment_block, row_offset = block_items
        return (key_step(kept, key_block, value_block, segment_block, row_offset), None)

    shaped = (
        key_piece.reshape(block_count, block_rows, -1),
        value_piece.reshape(block_count, block_rows, -1),
        segment_piece.reshape(block_count, block_rows),
        jnp.arange(block_count, dtype=jnp.int32) * block_rows,
    )
    result, unused = lax.scan(inner_step, start_state, shaped)
    final_max, denominator, weighted = result
    attended = weighted / denominator[..., None]
    return attended.transpose(2, 0, 1, 3).reshape(tok_rows, heads_local * HD).astype(jnp.bfloat16)


def solution(mesh):
    return jax.shard_map(
        per_device,
        mesh=mesh,
        in_specs=(
            P(("pool", "seq"), None),
            P(None, "seq"),
            P("seq", None),
            P(("pool", "seq")),
            P("seq", None),
            P("seq"),
            P("seq", "pool"),
            P("seq", "pool"),
            P("seq", "pool"),
        ),
        out_specs=P("seq", "pool"),
        check_vma=False,
    )
```

profile of v0, /device:TPU:6, one launch (start us, length us, event | category | flops | bytes accessed | tf_op | source)
XLA Modules:
  0.0 652.6 jit_solution(5322837525072245698)
XLA Ops:
  6.5 6.3 copy.71
  14.0 36.5 %all-gather.10.cloned.1.call-done = bf16[256,5120]{1,0:T(8,128)(2,1)} async-done(((bf16[16,5120]{1,0:T(8,128)(2,1)}), bf16[256,5120]{1,0:T(8,128)(2,1)}) %all-gather.10.cloned.1.call-update) | async-done | bytes 2621456 | tf_op jit(solution)/shard_map/all_gather | solution.py:50
  50.5 12.2 %fusion.41 = f32[256,8192]{1,0:T(8,128)} fusion(bf16[320,8192]{1,0:T(8,128)(2,1)} %param.13, bf16[256,5120]{1,0:T(8,128)(2,1)} %all-gather.10.cloned.1.call-done, bf16[5120,320]{0,1:T(8,128)(2,1)S(1)} %copy-done), kind=kOutput, calls=%fused_computation.74 | convolution fusion | flops 2186362880 | bytes 19529728 | tf_op jit(solution)/shard_map/dot_general | solution.py:57
  63.7 94.5 %reduce-scatter.2.cloned.1.call-done = f32[16,8192]{1,0:T(8,128)} async-done(((f32[256,8192]{1,0:T(8,128)}), f32[16,8192]{1,0:T(8,128)}) %reduce-scatter.2.cloned.1.call-update) | async-done | bytes 524304 | tf_op jit(solution)/shard_map/reduce_scatter | solution.py:56
  160.0 16.2 %all_to_all.14 = bf16[16,2,8192]{2,1,0:T(2,128)(2,1)} all-to-all(bf16[16,2,8192]{2,1,0:T(2,128)(2,1)S(1)} %reshape.340), channel_id=1, replica_groups=mesh['pool'=8,'seq'=16] {'seq'}, dimensions={0} | all-to-all | bytes 1048576 | tf_op jit(solution)/shard_map/all_to_all | solution.py:76
  178.7 5.7 all-to-all-start
  188.4 34.7 %all-gather = s32[128,1,2]{2,1,0:T(1,128)S(1)} all-gather(s32[16,1,2]{2,1,0:T(1,128)S(1)} %all-to-all-done), channel_id=2, replica_groups=mesh['pool'=8,'seq'=16] {'pool'}, dimensions={0}, use_global_device_ids=true | all-gather | bytes 1152 | tf_op jit(solution)/shard_map/all_gather | solution.py:81
  224.6 24.0 %all-gather.12.cloned.1.call-done = bf16[128,2,8192]{2,1,0:T(2,128)(2,1)} async-done(((bf16[16,2,8192]{2,1,0:T(2,128)(2,1)}), bf16[128,2,8192]{2,1,0:T(2,128)(2,1)}) %all-gather.12.cloned.1.call-update) | async-done | bytes 4194320 | tf_op jit(solution)/shard_map/all_gather | solution.py:80
  248.6 7.2 %reshape.350 = bf16[256,8192]{1,0:T(8,128)(2,1)} reshape(bf16[128,2,8192]{2,1,0:T(2,128)(2,1)} %all-gather.12.cloned.1.call-done) | data formatting | bytes 8388608 | tf_op jit(solution)/shard_map/reshape | solution.py:83
  255.8 14.2 %scatter_fusion = bf16[384,8192]{1,0:T(8,128)(2,1)} fusion(bf16[384,8192]{1,0:T(8,128)(2,1)} %copy.71, s32[256]{0:T(256)S(1)} %bitcast.114, bf16[256,8192]{1,0:T(8,128)(2,1)} %reshape.350), kind=kCustom, calls=%fused_computation | custom fusion | bytes 12583936 | tf_op jit(solution)/shard_map/scatter | solution.py:86
  274.2 6.6 %all-gather.14.cloned.1.call-done = bf16[8192,128]{1,0:T(8,128)(2,1)} async-done(((bf16[512,128]{1,0:T(8,128)(2,1)}), bf16[8192,128]{1,0:T(8,128)(2,1)}) %all-gather.14.cloned.1.call-update) | async-done | bytes 2097168 | tf_op jit(solution)/shard_map/all_gather | solution.py:90
  280.7 5.4 convolution_bitcast_fusion.1
  287.4 29.0 %all-gather.20.cloned.1.call-done = bf16[8192,128]{1,0:T(8,128)(2,1)} async-done(((bf16[512,128]{1,0:T(8,128)(2,1)}), bf16[8192,128]{1,0:T(8,128)(2,1)}) %all-gather.20.cloned.1.call-update) | async-done | bytes 2097168 | tf_op jit(solution)/shard_map/all_gather | solution.py:91
  316.4 5.9 convolution_convert_fusion.1
  322.3 16.1 %all-gather.1 = s32[16,1,384]{2,1,0:T(1,128)S(1)} all-gather(s32[1,1,384]{2,1,0:T(1,128)S(1)} %reshape.356), channel_id=1, replica_groups=mesh['pool'=8,'seq'=16] {'seq'}, dimensions={0}, use_global_device_ids=true | all-gather | bytes 26112 | tf_op jit(solution)/shard_map/all_gather | solution.py:152
  339.9 70.7 %all-gather.18.cloned.1.call-done = bf16[8192,1024]{1,0:T(8,128)(2,1)} async-done(((bf16[512,1024]{1,0:T(8,128)(2,1)}), bf16[8192,1024]{1,0:T(8,128)(2,1)}) %all-gather.18.cloned.1.call-update) | async-done | bytes 16777232 | tf_op jit(solution)/shard_map/all_gather | solution.py:89
  410.6 12.1 %convolution_bitcast_fusion = f32[48,8,8,128]{3,1,2,0:T(8,128)S(1)} fusion(bf16[8192,1024]{1,0:T(8,128)(2,1)} %all-gather.18.cloned.1.call-done, bf16[384,8192]{1,0:T(8,128)(2,1)} %scatter_fusion, f32[384]{0:T(512)S(1)} %add_rsqrt_fusion), kind=kOutput, calls=%fused_computation.40 | convolution fusion | flops 6451888128 | bytes 24643072 | tf_op jit(solution)/shard_map/dot_general | solution.py:95
  424.8 20.7 %all-gather.16.cloned.1.call-done = bf16[6144,128]{0,1:T(8,128)(2,1)} async-done(((bf16[384,128]{0,1:T(8,128)(2,1)}), bf16[6144,128]{0,1:T(8,128)(2,1)}) %all-gather.16.cloned.1.call-update) | async-done | bytes 1572880 | tf_op jit(solution)/shard_map/all_gather | solution.py:150
  447.4 33.0 %all-gather.22.cloned.1.call-done = bf16[6144,128]{1,0:T(8,128)(2,1)} async-done(((bf16[384,128]{1,0:T(8,128)(2,1)}), bf16[6144,128]{1,0:T(8,128)(2,1)}) %all-gather.22.cloned.1.call-update) | async-done | bytes 1572880 | tf_op jit(solution)/shard_map/all_gather | solution.py:151
  480.4 161.7 %while.15 = (s32[]{:T(128)}, f32[1,8,384]{2,1,0:T(8,128)S(1)}, f32[1,8,384]{2,1,0:T(8,128)S(1)}, f32[1,8,384,128]{3,2,1,0:T(8,128)}, s32[12]{0:T(128)S(1)}, /*in...) while((s32[]{:T(128)}, f32[1,8,384]{2,1,0:T(8,128)S(1)}, ...), condition=%wide.region_10.11_spmd.clone, body=%wide.region_7.10_spmd.clone.sunk | while | flops 827542400 | bytes 49233088 | solution.py:167
  485.7 6.1 bitcast_add_fusion.5
  498.8 6.6 %bitcast_add_fusion.5 = f32[1,8,384,128]{3,2,1,0:T(8,128)} fusion(f32[1,8,384,128]{3,2,1,0:T(8,128)} %get-tuple-element.242, f32[512,384,8]{1,0,2:T(8,128)} %get-tuple-element.224, f32[8,384]{1,0:T(8,128)S(1)} %bitcast.108, pred[384,512]{0,1:T(8,128)(4,1)S(1)} %compare_and_fusion.2, f32[8,384]{1,0:T(8,128)S(1)} %get-tuple-element.225, ...), kind=kOutput, calls=%fused_computation.10.clone.1 | convolution fusion | flops 411697152 | bytes 9789953 | tf_op jit(solution)/shard_map/while/body/eval_jaxpr/kgts,skd->kgtd/dot_general | solution.py:134
  512.3 6.6 %bitcast_add_fusion.5 = f32[1,8,384,128]{3,2,1,0:T(8,128)} fusion(f32[1,8,384,128]{3,2,1,0:T(8,128)} %get-tuple-element.242, f32[512,384,8]{1,0,2:T(8,128)} %get-tuple-element.224, f32[8,384]{1,0:T(8,128)S(1)} %bitcast.108, pred[384,512]{0,1:T(8,128)(4,1)S(1)} %compare_and_fusion.2, f32[8,384]{1,0:T(8,128)S(1)} %get-tuple-element.225, ...), kind=kOutput, calls=%fused_computation.10.clone.1 | convolution fusion | flops 411697152 | bytes 9789953 | tf_op jit(solution)/shard_map/while/body/eval_jaxpr/kgts,skd->kgtd/dot_general | solution.py:134
  525.8 6.6 %bitcast_add_fusion.5 = f32[1,8,384,128]{3,2,1,0:T(8,128)} fusion(f32[1,8,384,128]{3,2,1,0:T(8,128)} %get-tuple-element.242, f32[512,384,8]{1,0,2:T(8,128)} %get-tuple-element.224, f32[8,384]{1,0:T(8,128)S(1)} %bitcast.108, pred[384,512]{0,1:T(8,128)(4,1)S(1)} %compare_and_fusion.2, f32[8,384]{1,0:T(8,128)S(1)} %get-tuple-element.225, ...), kind=kOutput, calls=%fused_computation.10.clone.1 | convolution fusion | flops 411697152 | bytes 9789953 | tf_op jit(solution)/shard_map/while/body/eval_jaxpr/kgts,skd->kgtd/dot_general | solution.py:134
  539.3 6.6 %bitcast_add_fusion.5 = f32[1,8,384,128]{3,2,1,0:T(8,128)} fusion(f32[1,8,384,128]{3,2,1,0:T(8,128)} %get-tuple-element.242, f32[512,384,8]{1,0,2:T(8,128)} %get-tuple-element.224, f32[8,384]{1,0:T(8,128)S(1)} %bitcast.108, pred[384,512]{0,1:T(8,128)(4,1)S(1)} %compare_and_fusion.2, f32[8,384]{1,0:T(8,128)S(1)} %get-tuple-element.225, ...), kind=kOutput, calls=%fused_computation.10.clone.1 | convolution fusion | flops 411697152 | bytes 9789953 | tf_op jit(solution)/shard_map/while/body/eval_jaxpr/kgts,skd->kgtd/dot_general | solution.py:134
  552.8 6.6 %bitcast_add_fusion.5 = f32[1,8,384,128]{3,2,1,0:T(8,128)} fusion(f32[1,8,384,128]{3,2,1,0:T(8,128)} %get-tuple-element.242, f32[512,384,8]{1,0,2:T(8,128)} %get-tuple-element.224, f32[8,384]{1,0:T(8,128)S(1)} %bitcast.108, pred[384,512]{0,1:T(8,128)(4,1)S(1)} %compare_and_fusion.2, f32[8,384]{1,0:T(8,128)S(1)} %get-tuple-element.225, ...), kind=kOutput, calls=%fused_computation.10.clone.1 | convolution fusion | flops 411697152 | bytes 9789953 | tf_op jit(solution)/shard_map/while/body/eval_jaxpr/kgts,skd->kgtd/dot_general | solution.py:134
  566.3 6.6 %bitcast_add_fusion.5 = f32[1,8,384,128]{3,2,1,0:T(8,128)} fusion(f32[1,8,384,128]{3,2,1,0:T(8,128)} %get-tuple-element.242, f32[512,384,8]{1,0,2:T(8,128)} %get-tuple-element.224, f32[8,384]{1,0:T(8,128)S(1)} %bitcast.108, pred[384,512]{0,1:T(8,128)(4,1)S(1)} %compare_and_fusion.2, f32[8,384]{1,0:T(8,128)S(1)} %get-tuple-element.225, ...), kind=kOutput, calls=%fused_computation.10.clone.1 | convolution fusion | flops 411697152 | bytes 9789953 | tf_op jit(solution)/shard_map/while/body/eval_jaxpr/kgts,skd->kgtd/dot_general | solution.py:134
  579.9 6.6 %bitcast_add_fusion.5 = f32[1,8,384,128]{3,2,1,0:T(8,128)} fusion(f32[1,8,384,128]{3,2,1,0:T(8,128)} %get-tuple-element.242, f32[512,384,8]{1,0,2:T(8,128)} %get-tuple-element.224, f32[8,384]{1,0:T(8,128)S(1)} %bitcast.108, pred[384,512]{0,1:T(8,128)(4,1)S(1)} %compare_and_fusion.2, f32[8,384]{1,0:T(8,128)S(1)} %get-tuple-element.225, ...), kind=kOutput, calls=%fused_computation.10.clone.1 | convolution fusion | flops 411697152 | bytes 9789953 | tf_op jit(solution)/shard_map/while/body/eval_jaxpr/kgts,skd->kgtd/dot_general | solution.py:134
  593.4 6.6 %bitcast_add_fusion.5 = f32[1,8,384,128]{3,2,1,0:T(8,128)} fusion(f32[1,8,384,128]{3,2,1,0:T(8,128)} %get-tuple-element.242, f32[512,384,8]{1,0,2:T(8,128)} %get-tuple-element.224, f32[8,384]{1,0:T(8,128)S(1)} %bitcast.108, pred[384,512]{0,1:T(8,128)(4,1)S(1)} %compare_and_fusion.2, f32[8,384]{1,0:T(8,128)S(1)} %get-tuple-element.225, ...), kind=kOutput, calls=%fused_computation.10.clone.1 | convolution fusion | flops 411697152 | bytes 9789953 | tf_op jit(solution)/shard_map/while/body/eval_jaxpr/kgts,skd->kgtd/dot_general | solution.py:134
  606.9 6.6 %bitcast_add_fusion.5 = f32[1,8,384,128]{3,2,1,0:T(8,128)} fusion(f32[1,8,384,128]{3,2,1,0:T(8,128)} %get-tuple-element.242, f32[512,384,8]{1,0,2:T(8,128)} %get-tuple-element.224, f32[8,384]{1,0:T(8,128)S(1)} %bitcast.108, pred[384,512]{0,1:T(8,128)(4,1)S(1)} %compare_and_fusion.2, f32[8,384]{1,0:T(8,128)S(1)} %get-tuple-element.225, ...), kind=kOutput, calls=%fused_computation.10.clone.1 | convolution fusion | flops 411697152 | bytes 9789953 | tf_op jit(solution)/shard_map/while/body/eval_jaxpr/kgts,skd->kgtd/dot_general | solution.py:134
  620.4 6.6 %bitcast_add_fusion.5 = f32[1,8,384,128]{3,2,1,0:T(8,128)} fusion(f32[1,8,384,128]{3,2,1,0:T(8,128)} %get-tuple-element.242, f32[512,384,8]{1,0,2:T(8,128)} %get-tuple-element.224, f32[8,384]{1,0:T(8,128)S(1)} %bitcast.108, pred[384,512]{0,1:T(8,128)(4,1)S(1)} %compare_and_fusion.2, f32[8,384]{1,0:T(8,128)S(1)} %get-tuple-element.225, ...), kind=kOutput, calls=%fused_computation.10.clone.1 | convolution fusion | flops 411697152 | bytes 9789953 | tf_op jit(solution)/shard_map/while/body/eval_jaxpr/kgts,skd->kgtd/dot_general | solution.py:134
  633.9 6.6 %bitcast_add_fusion.5 = f32[1,8,384,128]{3,2,1,0:T(8,128)} fusion(f32[1,8,384,128]{3,2,1,0:T(8,128)} %get-tuple-element.242, f32[512,384,8]{1,0,2:T(8,128)} %get-tuple-element.224, f32[8,384]{1,0:T(8,128)S(1)} %bitcast.108, pred[384,512]{0,1:T(8,128)(4,1)S(1)} %compare_and_fusion.2, f32[8,384]{1,0:T(8,128)S(1)} %get-tuple-element.225, ...), kind=kOutput, calls=%fused_computation.10.clone.1 | convolution fusion | flops 411697152 | bytes 9789953 | tf_op jit(solution)/shard_map/while/body/eval_jaxpr/kgts,skd->kgtd/dot_general | solution.py:134
  (213 shorter events, 108.1 us)
Async XLA Ops:
  6.5 43.9 %copy-start = (bf16[5120,320]{0,1:T(8,128)(2,1)S(1)}, bf16[5120,320]{0,1:T(8,128)(2,1)}, u32[]{:S(2)}) copy-start(bf16[5120,320]{0,1:T(8,128)(2,1)} %param.12) | copy-start | bytes 9830404
  6.5 43.9 %all-gather.10.cloned.1.call-start = ((), (), s32[]{:S(2)}) async-start(), calls=%async_computation.3 | async-start | bytes 2785280 | tf_op jit(solution)/shard_map/all_gather | solution.py:50
  6.5 6.3 copy-start.4
  13.9 144.3 %reduce-scatter.2.cloned.1.call-start = ((), (), s32[]{:S(2)}) async-start(), calls=%async_computation.4 | async-start | bytes 8912896 | tf_op jit(solution)/shard_map/reduce_scatter | solution.py:56
  62.7 0.7 copy-start.6
  62.7 185.9 %all-gather.12.cloned.1.call-start = ((), (), s32[]{:S(2)}) async-start(), calls=%async_computation.5 | async-start | bytes 4718592 | tf_op jit(solution)/shard_map/all_gather | solution.py:80
  176.2 104.6 %all-gather.14.cloned.1.call-start = ((), (), s32[]{:S(2)}) async-start(), calls=%async_computation.6 | async-start | bytes 2228224 | tf_op jit(solution)/shard_map/all_gather | solution.py:90
  176.8 139.6 %all-gather.20.cloned.1.call-start = ((), (), s32[]{:S(2)}) async-start(), calls=%async_computation.9 | async-start | bytes 2228224 | tf_op jit(solution)/shard_map/all_gather | solution.py:91
  177.3 233.3 %all-gather.18.cloned.1.call-start = ((), (), s32[]{:S(2)}) async-start(), calls=%async_computation.8 | async-start | bytes 17825792 | tf_op jit(solution)/shard_map/all_gather | solution.py:89
  178.7 9.7 %all-to-all-start = ((s32[16,1,2]{2,1,0:T(1,128)}), s32[16,1,2]{2,1,0:T(1,128)S(1)}, u32[]{:S(2)}, u32[]{:S(2)}) async-start(s32[16,1,2]{2,1,0:T(1,128)} %bitcast), calls=%async_computation | async-start | bytes 16384 | tf_op jit(solution)/shard_map/all_to_all | solution.py:77
  184.4 261.0 %all-gather.16.cloned.1.call-start = ((), (), s32[]{:S(2)}) async-start(), calls=%async_computation.7 | async-start | bytes 1671168 | tf_op jit(solution)/shard_map/all_gather | solution.py:150
  274.2 13.2 %copy-start.5 = (s32[384]{0:T(512)S(1)}, s32[384]{0:T(512)}, u32[]{:S(2)}) copy-start(s32[384]{0:T(512)} %param.16) | copy-start | bytes 4612
  287.3 193.1 %all-gather.22.cloned.1.call-start = ((), (), s32[]{:S(2)}) async-start(), calls=%async_computation.10 | async-start | bytes 1671168 | tf_op jit(solution)/shard_map/all_gather | solution.py:151
  422.8 0.9 copy-start.3
  485.7 6.1 copy-start.2
  498.8 6.6 %copy-start.2 = (f32[512,384,8]{1,0,2:T(8,128)S(1)}, f32[512,384,8]{1,0,2:T(8,128)}, u32[]{:S(2)}) copy-start(f32[512,384,8]{1,0,2:T(8,128)} %get-tuple-element.224) | copy-start | bytes 18874372 | tf_op jit(solution)/shard_map/while
  512.3 6.6 %copy-start.2 = (f32[512,384,8]{1,0,2:T(8,128)S(1)}, f32[512,384,8]{1,0,2:T(8,128)}, u32[]{:S(2)}) copy-start(f32[512,384,8]{1,0,2:T(8,128)} %get-tuple-element.224) | copy-start | bytes 18874372 | tf_op jit(solution)/shard_map/while
  525.8 6.6 %copy-start.2 = (f32[512,384,8]{1,0,2:T(8,128)S(1)}, f32[512,384,8]{1,0,2:T(8,128)}, u32[]{:S(2)}) copy-start(f32[512,384,8]{1,0,2:T(8,128)} %get-tuple-element.224) | copy-start | bytes 18874372 | tf_op jit(solution)/shard_map/while
  539.3 6.6 %copy-start.2 = (f32[512,384,8]{1,0,2:T(8,128)S(1)}, f32[512,384,8]{1,0,2:T(8,128)}, u32[]{:S(2)}) copy-start(f32[512,384,8]{1,0,2:T(8,128)} %get-tuple-element.224) | copy-start | bytes 18874372 | tf_op jit(solution)/shard_map/while
  552.8 6.6 %copy-start.2 = (f32[512,384,8]{1,0,2:T(8,128)S(1)}, f32[512,384,8]{1,0,2:T(8,128)}, u32[]{:S(2)}) copy-start(f32[512,384,8]{1,0,2:T(8,128)} %get-tuple-element.224) | copy-start | bytes 18874372 | tf_op jit(solution)/shard_map/while
  566.3 6.6 %copy-start.2 = (f32[512,384,8]{1,0,2:T(8,128)S(1)}, f32[512,384,8]{1,0,2:T(8,128)}, u32[]{:S(2)}) copy-start(f32[512,384,8]{1,0,2:T(8,128)} %get-tuple-element.224) | copy-start | bytes 18874372 | tf_op jit(solution)/shard_map/while
  579.8 6.6 %copy-start.2 = (f32[512,384,8]{1,0,2:T(8,128)S(1)}, f32[512,384,8]{1,0,2:T(8,128)}, u32[]{:S(2)}) copy-start(f32[512,384,8]{1,0,2:T(8,128)} %get-tuple-element.224) | copy-start | bytes 18874372 | tf_op jit(solution)/shard_map/while
  593.4 6.6 %copy-start.2 = (f32[512,384,8]{1,0,2:T(8,128)S(1)}, f32[512,384,8]{1,0,2:T(8,128)}, u32[]{:S(2)}) copy-start(f32[512,384,8]{1,0,2:T(8,128)} %get-tuple-element.224) | copy-start | bytes 18874372 | tf_op jit(solution)/shard_map/while
  606.9 6.6 %copy-start.2 = (f32[512,384,8]{1,0,2:T(8,128)S(1)}, f32[512,384,8]{1,0,2:T(8,128)}, u32[]{:S(2)}) copy-start(f32[512,384,8]{1,0,2:T(8,128)} %get-tuple-element.224) | copy-start | bytes 18874372 | tf_op jit(solution)/shard_map/while
  620.4 6.6 %copy-start.2 = (f32[512,384,8]{1,0,2:T(8,128)S(1)}, f32[512,384,8]{1,0,2:T(8,128)}, u32[]{:S(2)}) copy-start(f32[512,384,8]{1,0,2:T(8,128)} %get-tuple-element.224) | copy-start | bytes 18874372 | tf_op jit(solution)/shard_map/while
  633.9 6.6 %copy-start.2 = (f32[512,384,8]{1,0,2:T(8,128)S(1)}, f32[512,384,8]{1,0,2:T(8,128)}, u32[]{:S(2)}) copy-start(f32[512,384,8]{1,0,2:T(8,128)} %get-tuple-element.224) | copy-start | bytes 18874372 | tf_op jit(solution)/shard_map/while
  642.1 3.6 copy-start.1
Sparse Core Ops, SparseCore 0:
  14.0 36.3 all-gather.9
  62.8 95.3 reduce-scatter.1
  176.3 72.2 all-gather.11
  250.2 30.5 all-gather.13
  282.3 34.0 all-gather.19
  317.9 92.6 all-gather.17
  412.3 33.1 all-gather.15
  447.2 33.1 all-gather.21
where the time goes:
time: 655 us; the launch traced here: 653 us
  waiting for transfers between devices  321 us (49%)
  matrix products  161 us (25%)
  blocking collectives  67 us (10%)
  local copies, waits for them, and re-layouts  42.4 us (6%)
  other arithmetic  40.5 us (6%)
  between operations  13.7 us (2%)
    reduce_scatter x1, waiting for transfers between devices, per_device(): lax.psum_scatter(jnp.dot(hidden, merge_down, preferred_element_type=jnp.f...  94.5 us
    dot_general x12, matrix products, block_update(): jnp.einsum('kgts,skd->kgtd', weights.astype(jnp.bfloat16), value_block.re...  78.7 us
    all_gather x1, waiting for transfers between devices, per_device(): lax.all_gather(query_weight, 'seq', axis=0, tiled=True)  70.7 us
    dot_general x12, matrix products, block_update(): jnp.einsum('tkgd,skd->kgts', queries, key_block.reshape(row_count, kv_loc...  45.6 us
    all_gather x1, waiting for transfers between devices, per_device(): lax.all_gather(merged, 'seq', axis=0, tiled=True)  36.5 us
    all_gather x1, blocking collectives, per_device(): lax.all_gather(got_offsets, 'pool', axis=0, tiled=True)  34.7 us
    all_gather x1, waiting for transfers between devices, per_device(): value_piece = lax.all_gather(values, 'seq', axis=0, tiled=True)  33 us
    all_gather x1, waiting for transfers between devices, per_device(): lax.all_gather(value_weight, 'seq', axis=0, tiled=True)  29 us
  transfers between devices with their start and end apart: 9, of which 9 were waited for; matrix products, arithmetic and copies ran while one was open for 9% of the time, Pallas kernels for 0%

commit v1 on v0

v1 whole, which is shorter than its diff:
```python
import functools

import jax
import jax.numpy as jnp
from jax import lax
from jax.experimental import pallas as pl
from jax.experimental.pallas import tpu as pltpu
from jax.sharding import PartitionSpec as P

HD = 128
CAP = 2
AUX = 128
NORM_EPS = 1e-06
ROPE_BASE = 1000000.0
BIG_NEG = -1e30
VMEM_BYTES = 56 * 1024 * 1024
X, Y, C = 4, 2, 2


def rms_rows(matrix):
    return matrix * lax.rsqrt(jnp.mean(matrix * matrix, axis=-1, keepdims=True) + NORM_EPS)


def seq_shift(array, dx, dy, dc):
    pairs = []
    for source in range(X * Y * C):
        x, y, c = source // (Y * C), source // C % Y, source % C
        pairs.append((source, ((x + dx) % X) * Y * C + (y ^ dy) * C + (c ^ dc)))
    return lax.ppermute(array, "seq", pairs)


OFFSETS = [(dx, dy) for dx in range(X) for dy in range(Y)]


def qkv_kernel(text_ref, slots_ref, weight_ref, cos_ref, sin_ref, out_ref, x_ref):
    rows, width = text_ref.shape
    slot_count = slots_ref.shape[0]
    step = pl.program_id(0)
    chunk = 1024

    @pl.when(step == 0)
    def _():
        aux = slots_ref[:, width:].astype(jnp.float32)
        offset = aux[:, 0:1] * 128.0 + aux[:, 1:2]
        offset = jnp.where(aux[:, 2:3] > 0.5, offset, -1.0).astype(jnp.int32)
        token = lax.broadcasted_iota(jnp.int32, (slot_count, rows), 1)
        select = jnp.where(offset == token, 1.0, 0.0).T.astype(jnp.bfloat16)
        held = jnp.dot(select, slots_ref[:, width:], preferred_element_type=jnp.float32)[:, 2:3] > 0.5
        total = jnp.zeros((rows, 1), jnp.float32)
        for start in range(0, width, chunk):
            part = slice(start, start + chunk)
            image = jnp.dot(select, slots_ref[:, part], preferred_element_type=jnp.float32)
            mixed = jnp.where(held, image, text_ref[:, part].astype(jnp.float32))
            total += jnp.sum(mixed * mixed, axis=1, keepdims=True)
            x_ref[:, part] = mixed.astype(jnp.bfloat16)
        scale = lax.rsqrt(total / width + NORM_EPS)
        for start in range(0, width, chunk):
            part = slice(start, start + chunk)
            x_ref[:, part] = (x_ref[:, part].astype(jnp.float32) * scale).astype(jnp.bfloat16)

    acc = jnp.dot(x_ref[...], weight_ref[...], preferred_element_type=jnp.float32)
    last = pl.num_programs(0) - 1
    cosine, sine = cos_ref[...], sin_ref[...]

    def turned(part):
        return part * cosine + pltpu.roll(part, HD // 2, 1) * sine

    out_ref[:, :HD] = turned(acc[:, :HD]).astype(jnp.bfloat16)

    @pl.when(step < last)
    def _():
        out_ref[:, HD:] = turned(acc[:, HD:]).astype(jnp.bfloat16)

    @pl.when(step == last)
    def _():
        out_ref[:, HD:] = acc[:, HD:].astype(jnp.bfloat16)


def project(text_rows, slots, weights, cosine, sine):
    rows, width = text_rows.shape
    columns = weights.shape[1]
    block = 2 * HD
    whole = lambda shape: pl.BlockSpec(shape, lambda n: (0, 0), pipeline_mode=pl.Buffered(1))
    return pl.pallas_call(
        qkv_kernel,
        grid=(columns // block,),
        in_specs=[
            whole((rows, width)),
            whole(slots.shape),
            pl.BlockSpec((width, block), lambda n: (0, n)),
            whole((rows, HD)),
            whole((rows, HD)),
        ],
        out_specs=pl.BlockSpec((rows, block), lambda n: (0, n)),
        out_shape=jax.ShapeDtypeStruct((rows, columns), jnp.bfloat16),
        scratch_shapes=[pltpu.VMEM((rows, width), jnp.bfloat16)],
        compiler_params=pltpu.CompilerParams(vmem_limit_bytes=VMEM_BYTES),
        name="project",
    )(text_rows, slots, weights, cosine, sine)


GROUP = 2


def attention_kernel(info_ref, q_ref, kv_ref, start_ref, out_ref, qs_ref, top_ref, sum_ref, acc_ref):
    rows = q_ref.shape[0]
    heads = out_ref.shape[1] // HD
    groups = heads // GROUP
    wide = GROUP * rows
    me = info_ref[0]
    first = info_ref[1]
    edge = info_ref[2]
    factor = HD ** (-0.5) * 1.4426950408889634
    for h in range(heads):
        qs_ref[h * rows:(h + 1) * rows, :] = q_ref[:, h * HD:(h + 1) * HD]

    def block(index, masked, fresh):
        keys = kv_ref[index, :, :HD]
        values = kv_ref[index, :, HD:]
        if masked:
            key_at = index * rows + lax.broadcasted_iota(jnp.int32, (rows, rows), 0)
            query_at = me * rows + lax.broadcasted_iota(jnp.int32, (rows, rows), 1)
            allowed = (key_at <= query_at) & (key_at >= start_ref[0:1, :])
            allowed = jnp.concatenate([allowed] * GROUP, axis=1)
        for g in range(groups):
            part = slice(g * wide, (g + 1) * wide)
            scores = lax.dot_general(
                keys, qs_ref[part, :], (((1,), (1,)), ((), ())), preferred_element_type=jnp.float32
            )
            if masked:
                scores = jnp.where(allowed, scores, BIG_NEG)
            top = jnp.max(scores, axis=0, keepdims=True)
            if not fresh:
                old = top_ref[:, part]
                top = jnp.maximum(old, top)
            probs = jnp.exp2((scores - top) * factor)
            total = jnp.sum(probs, axis=0, keepdims=True)
            mixed = lax.dot_general(
                values, probs.astype(jnp.bfloat16), (((0,), (0,)), ((), ())), preferred_element_type=jnp.float32
            )
            if not fresh:
                shrink = jnp.exp2((old - top) * factor)
                total += sum_ref[:, part] * shrink
                mixed += acc_ref[:, part] * shrink
            top_ref[:, part] = top
            sum_ref[:, part] = total
            acc_ref[:, part] = mixed

    block(me, True, True)

    def step(i, _):
        index = me - 1 - i
        needs = index * rows < edge

        @pl.when(needs)
        def _():
            block(index, True, False)

        @pl.when(jnp.logical_not(needs))
        def _():
            block(index, False, False)

        return 0

    lax.fori_loop(0, me - first, step, 0)
    for h in range(heads):
        part = slice(h * rows, (h + 1) * rows)
        out_ref[:, h * HD:(h + 1) * HD] = (acc_ref[:, part] / sum_ref[:, part]).T.astype(jnp.bfloat16)


def attend(info, qkv, kv_all, starts, heads):
    rows = qkv.shape[0]
    vmem = pl.BlockSpec(memory_space=pltpu.VMEM)
    return pl.pallas_call(
        attention_kernel,
        in_specs=[pl.BlockSpec(memory_space=pltpu.SMEM), vmem, vmem, vmem],
        out_specs=vmem,
        out_shape=jax.ShapeDtypeStruct((rows, heads * HD), jnp.bfloat16),
        scratch_shapes=[
            pltpu.VMEM((heads * rows, HD), jnp.bfloat16),
            pltpu.VMEM((1, heads * rows), jnp.float32),
            pltpu.VMEM((1, heads * rows), jnp.float32),
            pltpu.VMEM((HD, heads * rows), jnp.float32),
        ],
        compiler_params=pltpu.CompilerParams(vmem_limit_bytes=VMEM_BYTES),
        name="attend",
    )(info, qkv, kv_all, starts)


def per_device(
    patches,
    merge_up,
    merge_down,
    image_pos,
    text_rows,
    segment,
    query_weight,
    key_weight,
    value_weight,
):
    seq_count = lax.axis_size("seq")
    seq_index = lax.axis_index("seq")
    rows, width = text_rows.shape
    bf16, f32 = jnp.bfloat16, jnp.float32

    with jax.named_scope("weights"):
        weights = lax.all_gather(
            jnp.concatenate([query_weight, key_weight, value_weight], axis=1), "seq", axis=0, tiled=True
        )

    with jax.named_scope("merger_up"):
        normed = rms_rows(patches.astype(f32)).astype(bf16)
        merged = normed.reshape(-1, 4 * patches.shape[1])
        own, merged_width = merged.shape
        below = jnp.sum((segment[None, :] < jnp.arange(1, 4, dtype=jnp.int32)[:, None]).astype(jnp.int32), axis=1)
        counts = jnp.concatenate([below // 128, below % 128]).astype(bf16)
        counts = jnp.broadcast_to(jnp.pad(counts, (0, AUX - 6))[None, :], (own, AUX))
        merged = jnp.concatenate([merged, counts], axis=1)
        pieces = [merged if (dx, dy) == (0, 0) else seq_shift(merged, dx, dy, 0) for dx, dy in OFFSETS]
        mine = jnp.concatenate(pieces, axis=0)
        other = seq_shift(mine, 0, 0, 1)

        def up(block):
            return jax.nn.gelu(
                jnp.dot(block[:, :merged_width], merge_up, preferred_element_type=f32), approximate=False
            ).astype(bf16)

        counted = jnp.sum(
            mine[::own, merged_width:].astype(f32) + other[::own, merged_width:].astype(f32), axis=0
        )
        ends = (counted[:3] * 128.0 + counted[3:6]).astype(jnp.int32)
        hidden_other = up(other)
        hidden_mine = up(mine)

    with jax.named_scope("merger_down"):
        partial_other = jnp.dot(hidden_other, merge_down, preferred_element_type=f32).astype(bf16)
        received = seq_shift(partial_other, 0, 0, 1)
        partial = jnp.dot(hidden_mine, merge_down, preferred_element_type=f32) + received.astype(f32)
        partial = partial.reshape(X, Y * own, width)
        received = [seq_shift(partial[dx].astype(bf16), -dx, 0, 0) for dx in range(1, X)]
        partial = partial[0] + sum(piece.astype(f32) for piece in received)
        received = seq_shift(partial[own:].astype(bf16), 0, 1, 0)
        image_rows = (partial[:own] + received.astype(f32)).astype(bf16)

    with jax.named_scope("route"):
        target = image_pos // rows
        offset = image_pos % rows
        matches = (target[:, None] == jnp.arange(seq_count, dtype=jnp.int32)[None, :]).astype(jnp.int32)
        slot_rank = jnp.sum((jnp.cumsum(matches, axis=0) - matches) * matches, axis=1)
        slot_index = target * CAP + slot_rank
        select = (slot_index[None, :] == jnp.arange(seq_count * CAP, dtype=jnp.int32)[:, None]).astype(bf16)
        marks = jnp.stack([offset // 128, offset % 128, jnp.ones_like(offset)], axis=1).astype(bf16)
        marks = jnp.pad(marks, ((0, 0), (0, AUX - 3)))
        send = jnp.dot(
            select, jnp.concatenate([image_rows, marks], axis=1), preferred_element_type=f32
        ).astype(bf16)
        got = lax.all_to_all(
            send.reshape(seq_count, CAP, width + AUX), "seq", split_axis=0, concat_axis=0, tiled=True
        )
        slots = lax.all_gather(got, "pool", axis=0, tiled=True).reshape(-1, width + AUX)

    with jax.named_scope("project"):
        positions = (seq_index * rows + jnp.arange(rows, dtype=jnp.int32)).astype(f32)
        half = HD // 2
        frequency = ROPE_BASE ** (-(jnp.arange(half, dtype=f32) * 2.0 / HD))
        angles = positions[:, None] * frequency[None, :]
        cosine, sine = jnp.cos(angles), jnp.sin(angles)
        qkv = project(
            text_rows,
            slots,
            weights,
            jnp.concatenate([cosine, cosine], axis=1),
            jnp.concatenate([-sine, sine], axis=1),
        )
        q_columns = query_weight.shape[1]
        kv_all = lax.all_gather(qkv[:, q_columns:], "seq", axis=0, tiled=True)

    with jax.named_scope("attend"):
        before = jnp.concatenate([jnp.zeros((1,), jnp.int32), ends])
        starts = jnp.sum(
            jnp.where(segment[None, :] == jnp.arange(4, dtype=jnp.int32)[:, None], before[:, None], 0), axis=0
        )
        info = jnp.stack([seq_index, starts[0] // rows, starts[-1]]).astype(jnp.int32)
        return attend(
            info,
            qkv,
            kv_all.reshape(seq_count, rows, 2 * HD),
            starts[None, :],
            q_columns // HD,
        )


def solution(mesh):
    return jax.shard_map(
        per_device,
        mesh=mesh,
        in_specs=(
            P(("pool", "seq"), None),
            P(None, "seq"),
            P("seq", None),
            P(("pool", "seq")),
            P("seq", None),
            P("seq"),
            P("seq", "pool"),
            P("seq", "pool"),
            P("seq", "pool"),
        ),
        out_specs=P("seq", "pool"),
        check_vma=False,
    )
```

time: 655 us -> 410 us (0.63)
  matrix products: 161 us -> 19.2 us
  waiting for transfers between devices: 321 us -> 255 us
  Pallas kernels: 0 us -> 60.2 us
  blocking collectives: 67 us -> 14.5 us
  other arithmetic: 40.5 us -> 10.1 us
  local copies, waits for them, and re-layouts: 42.4 us -> 15.7 us
  starting transfers between devices: 6 us -> 15.2 us
    dot_general x29 -> x3, matrix products: 161 us -> 19.2 us  [the longest x1 10.4 us: per_device(): jnp.dot(hidden_mine, merge_down, preferred_element_type=f32)]
    reduce_scatter x1 -> x0, waiting for transfers between devices: 94.5 us -> none  [per_device(): lax.psum_scatter(jnp.dot(hidden, merge_down, preferred_element_type=jnp.f...]
    pallas_call x0 -> x2, Pallas kernels: none -> 60.2 us  [the longest x1 39.9 us: attend(): pl.pallas_call(attention_kernel, in_specs=[pl.BlockSpec(memory_space=pltp...]
    all_gather x2 -> x0, blocking collectives: 50.9 us -> none  [the longest x1 34.7 us: per_device(): lax.all_gather(got_offsets, 'pool', axis=0, tiled=True)]
    ppermute x0 -> x13, waiting for transfers between devices: none -> 50.2 us  [seq_shift(): return lax.ppermute(array, 'seq', pairs)]
    reduce_sum x13 -> x3, other arithmetic: 18.4 us -> 1.12 us  [the longest x1 1.01 us: per_device(): jnp.sum((segment[None, :] < jnp.arange(1, 4, dtype=jnp.int32)[:, None]).a...]
    all_gather x7 -> x3, waiting for transfers between devices: 221 us -> 205 us  [the longest x1 103 us: per_device(): lax.all_gather(jnp.concatenate([query_weight, key_weight, value_weight],...]
    ppermute x0 -> x13, starting transfers between devices: none -> 15.1 us  [seq_shift(): return lax.ppermute(array, 'seq', pairs)]
  transfers between devices with their start and end apart: 9 -> 16, of which waited for: 9 -> 14; matrix products, arithmetic and copies ran while one was open for 9% -> 4% of each run, Pallas kernels for 0% -> 0%
where the time goes in v1:
time: 410 us; the launch traced here: 405 us
  waiting for transfers between devices  255 us (62%)
  Pallas kernels  60.2 us (15%)
  matrix products  19.2 us (5%)
  local copies, waits for them, and re-layouts  15.7 us (4%)
  starting transfers between devices  15.2 us (4%)
  between operations  15.2 us (4%)
  blocking collectives  14.5 us (4%)
  other arithmetic  10.1 us (2%)
    all_gather x1, waiting for transfers between devices, per_device(): lax.all_gather(jnp.concatenate([query_weight, key_weight, value_weight],...  103 us
    all_gather x1, waiting for transfers between devices, per_device(): lax.all_gather(got, 'pool', axis=0, tiled=True).reshape(-1, width + AUX)  71.4 us
    ppermute x13, waiting for transfers between devices, seq_shift(): return lax.ppermute(array, 'seq', pairs)  50.2 us
    pallas_call x1, Pallas kernels, attend(): pl.pallas_call(attention_kernel, in_specs=[pl.BlockSpec(memory_space=pltp...  39.9 us
    all_gather x1, waiting for transfers between devices, per_device(): kv_all = lax.all_gather(qkv[:, q_columns:], 'seq', axis=0, tiled=True)  30 us
    pallas_call x1, Pallas kernels, project(): pl.pallas_call(qkv_kernel, grid=(columns // block,), in_specs=[whole((row...  20.3 us
    ppermute x13, starting transfers between devices, seq_shift(): return lax.ppermute(array, 'seq', pairs)  15.1 us
    all_to_all x1, blocking collectives, per_device(): lax.all_to_all(send.reshape(seq_count, CAP, width + AUX), 'seq', split_ax...  14.5 us
  transfers between devices with their start and end apart: 16, of which 14 were waited for; matrix products, arithmetic and copies ran while one was open for 4% of the time, Pallas kernels for 0%

profile of v1, /device:TPU:6, one launch (start us, length us, event | category | flops | bytes accessed | tf_op | source)
XLA Modules:
  0.0 405.1 jit_solution(9845000859898580081)
XLA Ops:
  8.6 1.7 fusion.7
  11.5 1.7 collective-permute-start
  13.6 1.4 collective-permute-start.2
  15.0 2.1 collective-permute-start.3
  17.1 2.4 collective-permute-start.4
  20.4 1.3 collective-permute-start.6
  21.6 2.3 collective-permute-done.2
  24.0 4.4 %collective-permute-done.4 = bf16[16,5248]{1,0:T(8,128)(2,1)S(1)} collective-permute-done((bf16[16,5248]{1,0:T(8,128)(2,1)S(1)}, bf16[16,5248]{1,0:T(8,128)(2,1)S(1)}, u32[]{:S(2)}, u32[]{:S(2)}) %collective-permute-start.4) | collective-permute-done | bytes 167968 | tf_op jit(solution)/shard_map/merger_up/ppermute | solution.py:29
  29.2 4.3 %collective-permute-done.6 = bf16[16,5248]{1,0:T(8,128)(2,1)S(1)} collective-permute-done((bf16[16,5248]{1,0:T(8,128)(2,1)S(1)}, bf16[16,5248]{1,0:T(8,128)(2,1)S(1)}, u32[]{:S(2)}, u32[]{:S(2)}) %collective-permute-start.6) | collective-permute-done | bytes 167968 | tf_op jit(solution)/shard_map/merger_up/ppermute | solution.py:29
  34.6 3.2 collective-permute-done.7
  37.8 8.5 %convolution_convert_fusion.1 = bf16[128,8192]{1,0:T(8,128)(2,1)} fusion(bf16[320,8192]{1,0:T(8,128)(2,1)} %param.11, bf16[5120,320]{0,1:T(8,128)(2,1)S(1)} %copy-done, bf16[128,5248]{1,0:T(8,128)(2,1)} %collective-permute-done.7), kind=kOutput, calls=%fused_computation.1 | convolution fusion | flops 1094230016 | bytes 11927552 | tf_op jit(solution)/shard_map/merger_down/dot_general | solution.py:236
  46.5 4.3 %collective-permute-done.8 = bf16[128,8192]{1,0:T(8,128)(2,1)} collective-permute-done((bf16[128,8192]{1,0:T(8,128)(2,1)}, bf16[128,8192]{1,0:T(8,128)(2,1)}, u32[]{:S(2)}, u32[]{:S(2)}) %collective-permute-start.8) | collective-permute-done | bytes 2097184 | tf_op jit(solution)/shard_map/merger_down/ppermute | solution.py:29
  50.9 10.4 %fusion.178 = (bf16[128,8192]{1,0:T(8,128)(2,1)}, f32[128,8192]{1,0:T(8,128)}) fusion(bf16[128,8192]{1,0:T(8,128)(2,1)} %collective-permute-done.8, bf16[320,8192]{1,0:T(8,128)(2,1)} %param.11, bf16[5120,320]{0,1:T(8,128)(2,1)S(1)} %copy-done, bf16[128,5248]{1,0:T(8,128)(2,1)} %copy-done.2), kind=kOutput, calls=%fused_computation.239 | convolution fusion | flops 1096327168 | bytes 18219008 | tf_op jit(solution)/shard_map/merger_down/dot_general | solution.py:238
  61.3 1.5 fusion.176
  62.7 1.6 collective-permute-start.11
  64.3 1.2 collective-permute-start.10
  66.6 11.0 %collective-permute-done.11 = bf16[32,8192]{1,0:T(8,128)(2,1)S(1)} collective-permute-done((bf16[32,8192]{1,0:T(8,128)(2,1)S(1)}, bf16[32,8192]{1,0:T(8,128)(2,1)S(1)}, u32[]{:S(2)}, u32[]{:S(2)}) %collective-permute-start.11) | collective-permute-done | bytes 524320 | tf_op jit(solution)/shard_map/merger_down/ppermute | solution.py:29
  77.6 3.1 collective-permute-done.10
  80.7 10.1 %collective-permute-done.9 = bf16[32,8192]{1,0:T(8,128)(2,1)S(1)} collective-permute-done((bf16[32,8192]{1,0:T(8,128)(2,1)S(1)}, bf16[32,8192]{1,0:T(8,128)(2,1)S(1)}, u32[]{:S(2)}, u32[]{:S(2)}) %collective-permute-start.9) | collective-permute-done | bytes 524320 | tf_op jit(solution)/shard_map/merger_down/ppermute | solution.py:29
  90.7 1.4 slice_add_fusion
  92.2 1.5 collective-permute-start.12
  94.0 6.5 %collective-permute-done.12 = bf16[16,8192]{1,0:T(8,128)(2,1)S(1)} collective-permute-done((bf16[16,8192]{1,0:T(8,128)(2,1)S(1)}, bf16[16,8192]{1,0:T(8,128)(2,1)S(1)}, u32[]{:S(2)}, u32[]{:S(2)}) %collective-permute-start.12) | collective-permute-done | bytes 262176 | tf_op jit(solution)/shard_map/merger_down/ppermute | solution.py:29
  101.1 14.5 %all_to_all.5 = bf16[16,2,8320]{2,1,0:T(2,128)(2,1)} all-to-all(bf16[16,2,8320]{2,1,0:T(2,128)(2,1)S(1)} %reshape.60), channel_id=1, replica_groups=mesh['pool'=8,'seq'=16] {'seq'}, dimensions={0} | all-to-all | bytes 1064960 | tf_op jit(solution)/shard_map/route/all_to_all | solution.py:257
  115.7 1.2 pad_maximum_fusion
  118.6 71.4 %all-gather.4.cloned.1.call-done = bf16[128,2,8320]{2,1,0:T(2,128)(2,1)} async-done(((bf16[16,2,8320]{2,1,0:T(2,128)(2,1)}), bf16[128,2,8320]{2,1,0:T(2,128)(2,1)}) %all-gather.4.cloned.1.call-update) | async-done | bytes 4259856 | tf_op jit(solution)/shard_map/route/all_gather | solution.py:260
  190.0 7.3 %reshape.61.slots_ref = bf16[256,8320]{1,0:T(8,128)(2,1)} reshape(bf16[128,2,8320]{2,1,0:T(2,128)(2,1)} %all-gather.4.cloned.1.call-done) | data formatting | bytes 8519680 | tf_op jit(solution)/shard_map/route/reshape | solution.py:260
  197.3 103.3 %all-gather.6.cloned.1.call-done.weight_ref = bf16[8192,1280]{1,0:T(8,128)(2,1)} async-done(((bf16[512,1280]{1,0:T(8,128)(2,1)}), bf16[8192,1280]{1,0:T(8,128)(2,1)}) %all-gather.6.cloned.1.call-update) | async-done | bytes 20971536 | tf_op jit(solution)/shard_map/weights/all_gather | solution.py:207
  300.6 20.3 %project.1.q_ref = bf16[384,1280]{1,0:T(8,128)(2,1)} custom-call(bf16[384,8192]{1,0:T(8,128)(2,1)} %text_ref.1, bf16[256,8320]{1,0:T(8,128)(2,1)} %reshape.61.slots_ref, bf16[8192,1280]{1,0:T(8,128)(2,1)} %all-gather.6.cloned.1.call-done.weight_ref, f32[384,128]{1,0:T(8,128)} %get-tuple-element.22.cos_ref, f32[384,128]{1,0:T(8,128)} %get-tuple-element.23.sin_ref), custom_call_target="tpu_custom_call" | custom-call | tf_op jit(solution)/shard_map/project/project/pallas_call | solution.py:84
  320.9 1.6 slice.76
  327.5 1.2 pad_add_fusion.1.info_ref
  328.6 30.0 %all-gather.8.cloned.1.call-done = bf16[6144,256]{1,0:T(8,128)(2,1)} async-done(((bf16[384,256]{1,0:T(8,128)(2,1)}), bf16[6144,256]{1,0:T(8,128)(2,1)}) %all-gather.8.cloned.1.call-update) | async-done | bytes 3145744 | tf_op jit(solution)/shard_map/project/all_gather | solution.py:276
  358.6 39.9 %attend.1 = bf16[384,1024]{1,0:T(8,128)(2,1)} custom-call(s32[3]{0:T(128)} %pad_add_fusion.1.info_ref, bf16[384,1280]{1,0:T(8,128)(2,1)} %project.1.q_ref, bf16[16,384,256]{2,1,0:T(8,128)(2,1)} %bitcast.14, s32[1,384]{1,0:T(1,128)} %broadcast_in_dim.15.start_ref), custom_call_target="tpu_custom_call" | custom-call | tf_op jit(solution)/shard_map/attend/attend/pallas_call | solution.py:174
  (72 shorter events, 13.4 us)
Async XLA Ops:
  6.5 31.3 %copy-start = (bf16[5120,320]{0,1:T(8,128)(2,1)S(1)}, bf16[5120,320]{0,1:T(8,128)(2,1)}, u32[]{:S(2)}) copy-start(bf16[5120,320]{0,1:T(8,128)(2,1)} %param.10) | copy-start | bytes 9830404
  6.5 183.5 %all-gather.4.cloned.1.call-start = ((), (), s32[]{:S(2)}) async-start(), calls=%async_computation.1 | async-start | bytes 4792320 | tf_op jit(solution)/shard_map/route/all_gather | solution.py:260
  11.5 8.1 %collective-permute-start = (bf16[16,5248]{1,0:T(8,128)(2,1)S(1)}, bf16[16,5248]{1,0:T(8,128)(2,1)S(1)}, u32[]{:S(2)}, u32[]{:S(2)}) collective-permute-start(bf16[16,5248]{1,0:T(8,128)(2,1)S(1)} %get-tuple-element.8), channel_id=1, source_target_pairs={{0,2},{1,3},{2,0},{3,1},{4,6},{5,7},{6,4},{7,5},{8,10},{9,11},{10,... | collective-permute-start | bytes 503816 | tf_op jit(solution)/shard_map/merger_up/ppermute | solution.py:29
  13.1 7.2 %collective-permute-start.1 = (bf16[16,5248]{1,0:T(8,128)(2,1)S(1)}, bf16[16,5248]{1,0:T(8,128)(2,1)S(1)}, u32[]{:S(2)}, u32[]{:S(2)}) collective-permute-start(bf16[16,5248]{1,0:T(8,128)(2,1)S(1)} %get-tuple-element.8), channel_id=1, source_target_pairs={{0,4},{1,5},{2,6},{3,7},{4,8},{5,9},{6,10},{7,11},{8,12},{9,13},{1... | collective-permute-start | bytes 503816 | tf_op jit(solution)/shard_map/merger_up/ppermute | solution.py:29
  13.6 10.3 %collective-permute-start.2 = (bf16[16,5248]{1,0:T(8,128)(2,1)S(1)}, bf16[16,5248]{1,0:T(8,128)(2,1)S(1)}, u32[]{:S(2)}, u32[]{:S(2)}) collective-permute-start(bf16[16,5248]{1,0:T(8,128)(2,1)S(1)} %get-tuple-element.8), channel_id=1, source_target_pairs={{0,6},{1,7},{2,4},{3,5},{4,10},{5,11},{6,8},{7,9},{8,14},{9,15},{1... | collective-permute-start | bytes 503816 | tf_op jit(solution)/shard_map/merger_up/ppermute | solution.py:29
  15.0 8.9 %collective-permute-start.3 = (bf16[16,5248]{1,0:T(8,128)(2,1)S(1)}, bf16[16,5248]{1,0:T(8,128)(2,1)S(1)}, u32[]{:S(2)}, u32[]{:S(2)}) collective-permute-start(bf16[16,5248]{1,0:T(8,128)(2,1)S(1)} %get-tuple-element.8), channel_id=1, source_target_pairs={{0,8},{1,9},{2,10},{3,11},{4,12},{5,13},{6,14},{7,15},{8,0},{9,1},... | collective-permute-start | bytes 503816 | tf_op jit(solution)/shard_map/merger_up/ppermute | solution.py:29
  17.1 11.3 %collective-permute-start.4 = (bf16[16,5248]{1,0:T(8,128)(2,1)S(1)}, bf16[16,5248]{1,0:T(8,128)(2,1)S(1)}, u32[]{:S(2)}, u32[]{:S(2)}) collective-permute-start(bf16[16,5248]{1,0:T(8,128)(2,1)S(1)} %get-tuple-element.8), channel_id=1, source_target_pairs={{0,10},{1,11},{2,8},{3,9},{4,14},{5,15},{6,12},{7,13},{8,2},{9,3},... | collective-permute-start | bytes 503816 | tf_op jit(solution)/shard_map/merger_up/ppermute | solution.py:29
  19.5 9.7 %collective-permute-start.5 = (bf16[16,5248]{1,0:T(8,128)(2,1)S(1)}, bf16[16,5248]{1,0:T(8,128)(2,1)S(1)}, u32[]{:S(2)}, u32[]{:S(2)}) collective-permute-start(bf16[16,5248]{1,0:T(8,128)(2,1)S(1)} %get-tuple-element.8), channel_id=1, source_target_pairs={{0,12},{1,13},{2,14},{3,15},{4,0},{5,1},{6,2},{7,3},{8,4},{9,5},{1... | collective-permute-start | bytes 503816 | tf_op jit(solution)/shard_map/merger_up/ppermute | solution.py:29
  20.4 13.1 %collective-permute-start.6 = (bf16[16,5248]{1,0:T(8,128)(2,1)S(1)}, bf16[16,5248]{1,0:T(8,128)(2,1)S(1)}, u32[]{:S(2)}, u32[]{:S(2)}) collective-permute-start(bf16[16,5248]{1,0:T(8,128)(2,1)S(1)} %get-tuple-element.8), channel_id=1, source_target_pairs={{0,14},{1,15},{2,12},{3,13},{4,2},{5,3},{6,0},{7,1},{8,6},{9,7},{1... | collective-permute-start | bytes 503816 | tf_op jit(solution)/shard_map/merger_up/ppermute | solution.py:29
  33.5 1.1 copy-start.2
  34.6 11.9 %copy-start.7 = (s32[16]{0:T(128)S(1)}, s32[16]{0:T(128)}, u32[]{:S(2)}) copy-start(s32[16]{0:T(128)} %param.12) | copy-start | bytes 196
  34.6 3.2 collective-permute-start.7
  46.4 4.5 %collective-permute-start.8 = (bf16[128,8192]{1,0:T(8,128)(2,1)}, bf16[128,8192]{1,0:T(8,128)(2,1)}, u32[]{:S(2)}, u32[]{:S(2)}) collective-permute-start(bf16[128,8192]{1,0:T(8,128)(2,1)} %convolution_convert_fusion.1), channel_id=1, source_target_pairs={{0,1},{1,0},{2,3},{3,2},{4,5},{5,4},{6,7},{7,6},{8,9},{9,8},{10,11... | collective-permute-start | bytes 6291464 | tf_op jit(solution)/shard_map/merger_down/ppermute | solution.py:29
  62.7 14.8 %collective-permute-start.11 = (bf16[32,8192]{1,0:T(8,128)(2,1)S(1)}, bf16[32,8192]{1,0:T(8,128)(2,1)S(1)}, u32[]{:S(2)}, u32[]{:S(2)}) collective-permute-start(bf16[32,8192]{1,0:T(8,128)(2,1)S(1)} %get-tuple-element.10), channel_id=1, source_target_pairs={{0,4},{1,5},{2,6},{3,7},{4,8},{5,9},{6,10},{7,11},{8,12},{9,13},{1... | collective-permute-start | bytes 1572872 | tf_op jit(solution)/shard_map/merger_down/ppermute | solution.py:29
  64.3 16.4 %collective-permute-start.10 = (bf16[32,8192]{1,0:T(8,128)(2,1)S(1)}, bf16[32,8192]{1,0:T(8,128)(2,1)S(1)}, u32[]{:S(2)}, u32[]{:S(2)}) collective-permute-start(bf16[32,8192]{1,0:T(8,128)(2,1)S(1)} %get-tuple-element.11), channel_id=1, source_target_pairs={{0,8},{1,9},{2,10},{3,11},{4,12},{5,13},{6,14},{7,15},{8,0},{9,1},... | collective-permute-start | bytes 1572872 | tf_op jit(solution)/shard_map/merger_down/ppermute | solution.py:29
  65.5 25.2 %collective-permute-start.9 = (bf16[32,8192]{1,0:T(8,128)(2,1)S(1)}, bf16[32,8192]{1,0:T(8,128)(2,1)S(1)}, u32[]{:S(2)}, u32[]{:S(2)}) collective-permute-start(bf16[32,8192]{1,0:T(8,128)(2,1)S(1)} %get-tuple-element.9), channel_id=1, source_target_pairs={{0,12},{1,13},{2,14},{3,15},{4,0},{5,1},{6,2},{7,3},{8,4},{9,5},{1... | collective-permute-start | bytes 1572872 | tf_op jit(solution)/shard_map/merger_down/ppermute | solution.py:29
  92.2 8.3 %collective-permute-start.12 = (bf16[16,8192]{1,0:T(8,128)(2,1)S(1)}, bf16[16,8192]{1,0:T(8,128)(2,1)S(1)}, u32[]{:S(2)}, u32[]{:S(2)}) collective-permute-start(bf16[16,8192]{1,0:T(8,128)(2,1)S(1)} %slice.98), channel_id=1, source_target_pairs={{0,2},{1,3},{2,0},{3,1},{4,6},{5,7},{6,4},{7,5},{8,10},{9,11},{10,... | collective-permute-start | bytes 786440 | tf_op jit(solution)/shard_map/merger_down/ppermute | solution.py:29
  100.9 14.8 %copy-start.3 = (bf16[512,1024]{1,0:T(8,128)(2,1)S(1)}, bf16[512,1024]{1,0:T(8,128)(2,1)}, u32[]{:S(2)}) copy-start(bf16[512,1024]{1,0:T(8,128)(2,1)} %param.15) | copy-start | bytes 3145732
  100.9 14.8 %copy-start.4 = (bf16[512,128]{1,0:T(8,128)(2,1)S(1)}, bf16[512,128]{1,0:T(8,128)(2,1)}, u32[]{:S(2)}) copy-start(bf16[512,128]{1,0:T(8,128)(2,1)} %param.17) | copy-start | bytes 393220
  100.9 14.8 %copy-start.5 = (bf16[512,128]{1,0:T(8,128)(2,1)S(1)}, bf16[512,128]{1,0:T(8,128)(2,1)}, u32[]{:S(2)}) copy-start(bf16[512,128]{1,0:T(8,128)(2,1)} %param.16) | copy-start | bytes 393220
  115.6 185.0 %all-gather.6.cloned.1.call-start = ((), (), s32[]{:S(2)}) async-start(), calls=%async_computation.2 | async-start | bytes 22282240 | tf_op jit(solution)/shard_map/weights/all_gather | solution.py:207
  116.9 241.7 %all-gather.8.cloned.1.call-start = ((), (), s32[]{:S(2)}) async-start(), calls=%async_computation.3 | async-start | bytes 3342336 | tf_op jit(solution)/shard_map/project/all_gather | solution.py:276
  300.6 23.7 %copy-start.6 = (s32[384]{0:T(512)S(1)}, s32[384]{0:T(512)}, u32[]{:S(2)}) copy-start(s32[384]{0:T(512)} %param.14) | copy-start | bytes 4612
  358.6 39.9 %copy-start.1 = (bf16[5120,320]{0,1:T(8,128)(2,1)S(1)}, bf16[5120,320]{0,1:T(8,128)(2,1)}, u32[]{:S(2)}) copy-start(bf16[5120,320]{0,1:T(8,128)(2,1)} %param.10) | copy-start | bytes 9830404
Sparse Core Ops, SparseCore 0:
  115.7 74.2 all-gather.3
  191.7 108.8 all-gather.5
  322.7 35.8 all-gather.7
